TPU v7x, 32 devices: a whole 2x2x4 slice. The times are simulated.
32 devices in a mesh: seq: 16 (over z, y, x), head: 2 (over core).
Axes of the slice: x: 2, y: 2, z: 4, core: 2. Of those that a mesh axis runs over, the one named last changes fastest.
Arguments:
- q_lin: bfloat16 [4096, 512], P('seq', 'head'), may hold values from -6 to 6
- k_lin: bfloat16 [4096, 512], P('seq', 'head'), may hold values from -6 to 6
- v_lin: bfloat16 [4096, 512], P('seq', 'head'), may hold values from -6 to 6
- log_decay: float32 [4, 4096], P('head', 'seq'), may hold values from -0.4 to 0, as said below
- q_soft: bfloat16 [4096, 512], P('seq', 'head'), may hold values from -12 to 12
- k_soft: bfloat16 [4096, 512], P('seq', 'head'), may hold values from -6 to 6
- v_soft: bfloat16 [4096, 512], P('seq', 'head'), may hold values from -6 to 6
- wo_lin: bfloat16 [512, 4096], P('head'), may hold values from -0.375 to 0.375
- wo_soft: bfloat16 [512, 4096], P('head'), may hold values from -0.375 to 0.375
Outputs:
- lin_mixed: bfloat16 [4096, 4096], P('seq', 'head')
- soft_mixed: bfloat16 [4096, 4096], P('seq', 'head')
Inputs may be any that keep to these rules, and one draw needn't show every extreme that they name: `log_decay`: log decays are never positive.
All inputs are finite; a program needn't handle non-finite values.
Results may differ from a plain program's by a relative error of at most 0.012.
Values may be sent and summed in bfloat16 or wider, within the bound.
A program may use at most 64 MiB of HBM per device.

v0:
```python
import math
import jax
import jax.numpy as jnp
from jax import lax
from jax.sharding import PartitionSpec as P

HIGHEST = lax.Precision.HIGHEST
NEG_BIG = -1e30


def prefix(shard, axis, combine, identity):
    size, here = (lax.axis_size(axis), lax.axis_index(axis))
    everything = jax.tree.map(
        lambda part, kind: lax.all_gather(part.astype(kind), axis),
        shard,
        (jnp.bfloat16, jnp.bfloat16),
    )
    start = jax.tree.map(
        lambda part, zero: jnp.broadcast_to(jnp.asarray(zero, part.dtype), part.shape),
        shard,
        identity,
    )

    def turn(k, before):
        reached = k < here
        new = combine(
            before, jax.tree.map(lambda part, own: part[k].astype(own.dtype), everything, shard)
        )
        return jax.tree.map(lambda a, b: jnp.where(reached, a, b), new, before)

    return lax.fori_loop(0, size, turn, start)


def second_half(device):
    return 2 * device + 1


def absorb(state, query_half, key_block, value_block, allowed, factor):
    row_top, row_sum, weighted = state
    scores = (
        jnp.einsum("qhd,khd->hqk", query_half, key_block, preferred_element_type=jnp.float32)
        * factor
    )
    if allowed is not None:
        scores = jnp.where(allowed[None], scores, -jnp.inf)
    new_top = jnp.maximum(row_top, jnp.max(scores, axis=-1))
    shrink = jnp.exp(row_top - new_top)
    weights = jnp.exp(scores - new_top[:, :, None])
    row_sum = row_sum * shrink + jnp.sum(weights, axis=-1)
    weighted = weighted * shrink.T[:, :, None] + jnp.einsum(
        "hqk,khd->qhd",
        weights.astype(jnp.bfloat16),
        value_block,
        preferred_element_type=jnp.float32,
    )
    return (new_top, row_sum, weighted)


def lightning_heads(q_lin, k_lin, v_lin, log_decay):
    row_count = q_lin.shape[0]
    head_count = log_decay.shape[0]
    head_width = q_lin.shape[1] // head_count
    query_plain = q_lin.reshape(row_count, head_count, head_width)
    key_plain = k_lin.reshape(row_count, head_count, head_width)
    queries = query_plain.astype(jnp.float32)
    key_rows = key_plain.astype(jnp.float32)
    values = v_lin.astype(jnp.float32).reshape(row_count, head_count, head_width)
    cumulative = jnp.cumsum(log_decay, axis=1)
    lower = jnp.arange(row_count)[:, None] >= jnp.arange(row_count)[None, :]
    decay_gap = jnp.where(lower[None], cumulative[:, :, None] - cumulative[:, None, :], -jnp.inf)
    scores = jnp.einsum(
        "thd,shd->hts", query_plain, key_plain, preferred_element_type=jnp.float32
    ) * jnp.exp(decay_gap)
    inside = jnp.einsum("hts,shd->thd", scores, values, precision=HIGHEST)
    closing = jnp.exp(cumulative[:, -1:] - cumulative)
    own_state = jnp.einsum(
        "shd,she->hde", key_rows * closing.T[:, :, None], values, precision=HIGHEST
    )
    own_decay = cumulative[:, -1]

    def combine(earlier, later):
        return (jnp.exp(later[1])[:, None, None] * earlier[0] + later[0], earlier[1] + later[1])

    identity = (jnp.zeros_like(own_state), jnp.zeros_like(own_decay))
    carried, _ = prefix((own_state, own_decay), "seq", combine, identity)
    from_before = (
        jnp.einsum("thd,hde->the", queries, carried, precision=HIGHEST)
        * jnp.exp(cumulative).T[:, :, None]
    )
    raw = inside + from_before
    factor = lax.rsqrt(jnp.mean(raw * raw, axis=-1, keepdims=True) + 1e-06)
    return (raw * factor).astype(jnp.bfloat16).reshape(row_count, head_count * head_width)


def softmax_heads(q_soft, k_soft, v_soft, head_width):
    row_count = q_soft.shape[0]
    half_rows = row_count // 2
    head_count = q_soft.shape[1] // head_width
    own_index = lax.axis_index("seq")
    factor = 1.0 / math.sqrt(head_width)
    shaped = q_soft.reshape(2, half_rows, head_count, head_width)
    query_ids = (2 * own_index, second_half(own_index))
    triangle = jnp.arange(half_rows)[:, None] >= jnp.arange(half_rows)[None, :]

    def block_pass(state, side, key_block, value_block, key_id):

        def full_block(inner_state):
            return absorb(inner_state, shaped[side], key_block, value_block, None, factor)

        def diagonal_block(inner_state):
            return absorb(inner_state, shaped[side], key_block, value_block, triangle, factor)

        def skipped(inner_state):
            return inner_state

        def not_below(inner_state):
            return lax.cond(key_id == query_ids[side], diagonal_block, skipped, inner_state)

        return lax.cond(key_id < query_ids[side], full_block, not_below, state)

    start_state = tuple(
        (
            (
                jnp.full((head_count, half_rows), NEG_BIG, jnp.float32),
                jnp.zeros((head_count, half_rows), jnp.float32),
                jnp.zeros((half_rows, head_count, head_width), jnp.float32),
            )
            for side in range(2)
        )
    )
    carry = start_state
    key_piece = lax.all_gather(k_soft, "seq", axis=0, tiled=True)
    value_piece = lax.all_gather(v_soft, "seq", axis=0, tiled=True)
    piece_rows = key_piece.shape[0]
    blocks = piece_rows // half_rows
    key_blocks = key_piece.reshape(blocks, half_rows, head_count, head_width)
    value_blocks = value_piece.reshape(blocks, half_rows, head_count, head_width)
    firsts = half_rows * jnp.arange(blocks, dtype=jnp.int32)

    def inner(state, block_item):
        key_block, value_block, first = block_item
        key_id = first // half_rows
        return (
            tuple(
                (block_pass(state[side], side, key_block, value_block, key_id) for side in range(2))
            ),
            None,
        )

    carry, _ = lax.scan(inner, carry, (key_blocks, value_blocks, firsts))
    halves = [
        (carry[side][2] / carry[side][1].T[:, :, None])
        .astype(jnp.bfloat16)
        .reshape(half_rows, head_count * head_width)
        for side in range(2)
    ]
    return jnp.concatenate(halves, axis=0)


def local(q_lin, k_lin, v_lin, log_decay, q_soft, k_soft, v_soft, wo_lin, wo_soft):
    head_width = q_lin.shape[1] // log_decay.shape[0]
    lin_out = lightning_heads(q_lin, k_lin, v_lin, log_decay)
    soft_out = softmax_heads(q_soft, k_soft, v_soft, head_width)
    lin_term = jnp.dot(lin_out, wo_lin, preferred_element_type=jnp.float32)
    soft_term = jnp.dot(soft_out, wo_soft, preferred_element_type=jnp.float32)
    lin_sum, soft_sum = (
        lax.psum_scatter(
            lin_term.astype(jnp.bfloat16).astype(jnp.float32).astype(jnp.bfloat16),
            "head",
            scatter_dimension=1,
            tiled=True,
        ).astype(jnp.float32),
        lax.psum_scatter(
            soft_term.astype(jnp.bfloat16).astype(jnp.float32).astype(jnp.bfloat16),
            "head",
            scatter_dimension=1,
            tiled=True,
        ).astype(jnp.float32),
    )
    return (lin_sum.astype(jnp.bfloat16), soft_sum.astype(jnp.bfloat16))


def solution(mesh):
    in_specs = (
        P("seq", "head"),
        P("seq", "head"),
        P("seq", "head"),
        P("head", "seq"),
        P("seq", "head"),
        P("seq", "head"),
        P("seq", "head"),
        P("head", None),
        P("head", None),
    )
    out_specs = (P("seq", "head"), P("seq", "head"))
    return jax.shard_map(local, mesh=mesh, in_specs=in_specs, out_specs=out_specs, check_vma=False)
```

profile of v0, /device:TPU:0, one launch (start us, length us, event | category | flops | bytes accessed | tf_op | source)
XLA Modules:
  0.0 389.1 jit_solution(17133437121583700277)
XLA Ops:
  9.3 1.0 copy.69
  10.4 1.8 convolution_convert_fusion.2
  13.8 1.2 dynamic-slice
  15.9 43.7 %all-reduce = bf16[32]{0:T(256)(128)(2,1)S(1)} all-reduce(bf16[32]{0:T(256)(128)(2,1)S(1)} %dynamic-update-slice), channel_id=2, replica_groups=mesh['seq'=16,'head'=2] {'seq'}, use_global_device_ids=true, to_apply=%add | all-reduce | flops 32 | bytes 128
  59.7 1.0 reshape.130
  60.7 1.1 convolution_multiply_fusion.4
  61.8 8.6 %all-gather.10.cloned.1.call-done = bf16[32,128,128]{2,1,0:T(8,128)(2,1)} async-done(((bf16[2,128,128]{2,1,0:T(8,128)(2,1)}), bf16[32,128,128]{2,1,0:T(8,128)(2,1)}) %all-gather.10.cloned.1.call-update) | async-done | bytes 1048592 | tf_op jit(solution)/shard_map/all_gather | solution.py:14
  70.5 15.6 %while.39 = (s32[]{:T(128)}, f32[2,128,128]{2,1,0:T(8,128)S(1)}, s32[]{:T(128)}, bf16[16,2]{1,0:T(8,128)(2,1)S(1)}, bf16[16,2,128,128]{3,2,1,0:T(8,128)(2,1)}, /*index=5*/s32[]{:T(128)}, s32[]{:T(128)}) while((s32[]{:T(128)}, f32[2,128,128]{2,1,0:T(8,128)S(1)}, s32[]{:T(128)}, bf16[16,2]{1,0:T(8,128)(2,1)S(1)}, ...), condition=%wide.region_3.4_spmd.clone, body=%wide.region_2.3_spmd.clone.sunk | while | flops 163846 | bytes 327813 | solution.py:31
  86.9 2.1 convolution_convert_fusion.1
  89.1 43.7 %all-gather.6.cloned.1.call-done = bf16[4096,256]{1,0:T(8,128)(2,1)} async-done(((bf16[256,256]{1,0:T(8,128)(2,1)}), bf16[4096,256]{1,0:T(8,128)(2,1)}) %all-gather.6.cloned.1.call-update) | async-done | bytes 2097168 | tf_op jit(solution)/shard_map/all_gather | solution.py:132
  132.8 4.0 %reshape.143 = bf16[32,128,2,128]{3,2,1,0:T(2,128)(2,1)} reshape(bf16[4096,256]{1,0:T(8,128)(2,1)} %all-gather.6.cloned.1.call-done) | data formatting | bytes 4194304 | tf_op jit(solution)/shard_map/reshape | solution.py:136
  136.8 58.2 %all-gather.8.cloned.1.call-done = bf16[4096,256]{1,0:T(8,128)(2,1)} async-done(((bf16[256,256]{1,0:T(8,128)(2,1)}), bf16[4096,256]{1,0:T(8,128)(2,1)}) %all-gather.8.cloned.1.call-update) | async-done | bytes 2097168 | tf_op jit(solution)/shard_map/all_gather | solution.py:133
  195.0 4.0 %reshape.144 = bf16[32,128,2,128]{3,2,1,0:T(2,128)(2,1)} reshape(bf16[4096,256]{1,0:T(8,128)(2,1)} %all-gather.8.cloned.1.call-done) | data formatting | bytes 4194304 | tf_op jit(solution)/shard_map/reshape | solution.py:137
  199.0 141.2 %while.38 = (s32[]{:T(128)}, f32[2,128]{1,0:T(2,128)S(1)}, f32[2,128]{1,0:T(2,128)S(1)}, f32[128,2,128]{2,0,1:T(8,128)S(1)}, f32[2,128]{1,0:T(2,128)S(1)}, /*ind...) while((s32[]{:T(128)}, f32[2,128]{1,0:T(2,128)S(1)}, ...), condition=%wide.region_23.24_spmd.clone.clone, body=%wide.region_6.23_spmd.clone.clone.sunk | while | flops 34162200 | bytes 2311003 | solution.py:150
  202.3 1.0 constant_dynamic-slice_fusion.3
  207.7 1.0 constant_dynamic-slice_fusion.3
  212.6 1.0 constant_dynamic-slice_fusion.3
  216.9 1.0 constant_dynamic-slice_fusion.3
  221.3 1.0 constant_dynamic-slice_fusion.3
  225.7 1.0 constant_dynamic-slice_fusion.3
  230.0 1.0 constant_dynamic-slice_fusion.3
  234.4 1.0 constant_dynamic-slice_fusion.3
  238.7 1.0 constant_dynamic-slice_fusion.3
  243.1 1.0 constant_dynamic-slice_fusion.3
  247.5 1.0 constant_dynamic-slice_fusion.3
  251.8 1.0 constant_dynamic-slice_fusion.3
  256.2 1.0 constant_dynamic-slice_fusion.3
  260.5 1.0 constant_dynamic-slice_fusion.3
  264.9 1.0 constant_dynamic-slice_fusion.3
  269.3 1.0 constant_dynamic-slice_fusion.3
  273.6 1.0 constant_dynamic-slice_fusion.3
  278.0 1.0 constant_dynamic-slice_fusion.3
  282.4 1.0 constant_dynamic-slice_fusion.3
  286.7 1.0 constant_dynamic-slice_fusion.3
  291.1 1.0 constant_dynamic-slice_fusion.3
  295.4 1.0 constant_dynamic-slice_fusion.3
  299.8 1.0 constant_dynamic-slice_fusion.3
  304.2 1.0 constant_dynamic-slice_fusion.3
  308.5 1.0 constant_dynamic-slice_fusion.3
  312.9 1.0 constant_dynamic-slice_fusion.3
  317.2 1.0 constant_dynamic-slice_fusion.3
  321.6 1.0 constant_dynamic-slice_fusion.3
  326.0 1.0 constant_dynamic-slice_fusion.3
  330.3 1.0 constant_dynamic-slice_fusion.3
  334.7 1.0 constant_dynamic-slice_fusion.3
  339.1 1.0 constant_dynamic-slice_fusion.3
  340.4 3.6 convolution_convert_fusion
  344.1 38.5 %reduce-scatter.5.cloned.1.call-done = bf16[256,2048]{1,0:T(8,128)(2,1)} async-done(((bf16[256,4096]{1,0:T(8,128)(2,1)}), bf16[256,2048]{1,0:T(8,128)(2,1)}) %reduce-scatter.5.cloned.1.call-update) | async-done | bytes 1048592 | tf_op jit(solution)/shard_map/reduce_scatter | solution.py:173
  (353 shorter events, 48.1 us)
Async XLA Ops:
  7.2 79.8 %copy-start = (bf16[256,4096]{1,0:T(8,128)(2,1)S(1)}, bf16[256,4096]{1,0:T(8,128)(2,1)}, u32[]{:S(2)}) copy-start(bf16[256,4096]{1,0:T(8,128)(2,1)} %param.28) | copy-start | bytes 6291460
  7.2 63.3 %all-gather.10.cloned.1.call-start = ((), (), s32[]{:S(2)}) async-start(), calls=%async_computation.6 | async-start | bytes 1114112 | tf_op jit(solution)/shard_map/all_gather | solution.py:14
  10.3 75.7 %copy-start.2 = (bf16[256,256]{1,0:T(8,128)(2,1)S(1)}, bf16[256,256]{1,0:T(8,128)(2,1)}, u32[]{:S(2)}) copy-start(bf16[256,256]{1,0:T(8,128)(2,1)} %param.21) | copy-start | bytes 393220
  12.2 120.6 %all-gather.6.cloned.1.call-start = ((), (), s32[]{:S(2)}) async-start(), calls=%async_computation.3 | async-start | bytes 2228224 | tf_op jit(solution)/shard_map/all_gather | solution.py:132
  13.0 73.4 %copy-start.1 = (bf16[256,256]{1,0:T(8,128)(2,1)S(1)}, bf16[256,256]{1,0:T(8,128)(2,1)}, u32[]{:S(2)}) copy-start(bf16[256,256]{1,0:T(8,128)(2,1)} %param.23) | copy-start | bytes 393220
  13.0 182.0 %all-gather.8.cloned.1.call-start = ((), (), s32[]{:S(2)}) async-start(), calls=%async_computation.4 | async-start | bytes 2228224 | tf_op jit(solution)/shard_map/all_gather | solution.py:133
  13.7 330.4 %reduce-scatter.3.cloned.1.call-start = ((), (), s32[]{:S(2)}) async-start(), calls=%async_computation.2 | async-start | bytes 3145728 | tf_op jit(solution)/shard_map/reduce_scatter | solution.py:167
  89.0 293.5 %reduce-scatter.5.cloned.1.call-start = ((), (), s32[]{:S(2)}) async-start(), calls=%async_computation.5 | async-start | bytes 3145728 | tf_op jit(solution)/shard_map/reduce_scatter | solution.py:173
Sparse Core Ops, SparseCore 0:
  12.3 58.0 all-gather.9
  73.2 59.5 all-gather.5
  135.6 59.3 all-gather.7
  197.6 8.2 reduce-scatter.2
  344.2 38.3 reduce-scatter.4
where the time goes:
time: 393 us; the launch traced here: 389 us
  waiting for transfers between devices  150 us (38%)
  loops' own time  89.1 us (23%)
  local copies, waits for them, and re-layouts  63.5 us (16%)
  blocking collectives  43.7 us (11%)
  other arithmetic  16.9 us (4%)
  between operations  14.6 us (4%)
  matrix products  10.7 us (3%)
    another operation x1, loops' own time, softmax_heads(): carry, _ = lax.scan(inner, carry, (key_blocks, value_blocks, firsts))  85.6 us
    all_gather x1, waiting for transfers between devices, softmax_heads(): value_piece = lax.all_gather(v_soft, 'seq', axis=0, tiled=True)  58.2 us
    dynamic_slice x128, local copies, waits for them, and re-layouts, softmax_heads(): carry, _ = lax.scan(inner, carry, (key_blocks, value_blocks, firsts))  50.6 us
    all_gather x1, waiting for transfers between devices, softmax_heads(): key_piece = lax.all_gather(k_soft, 'seq', axis=0, tiled=True)  43.7 us
    unnamed x1, blocking collectives  43.7 us
    reduce_scatter x1, waiting for transfers between devices, local(): lax.psum_scatter(soft_term.astype(jnp.bfloat16).astype(jnp.float32).astyp...  38.5 us
    select_n x16, other arithmetic, turn(): return jax.tree.map(lambda a, b: jnp.where(reached, a, b), new, before)  14.9 us
    all_gather x1, waiting for transfers between devices, prefix(): lax.all_gather(part.astype(kind), axis)  8.65 us
  transfers between devices with their start and end apart: 5, of which 4 were waited for; matrix products, arithmetic and copies ran while one was open for 22% of the time, Pallas kernels for 0%

commit v1 on v0

--- a/solution.py
+++ b/solution.py
@@ -6,6 +6,24 @@
 
 HIGHEST = lax.Precision.HIGHEST
 NEG_BIG = -1e30
+
+
+def collect(value, axis, dim):
+    ways, here, step = (lax.axis_size(axis), lax.axis_index(axis), value.shape[dim])
+    dims = [n * ways if d == dim else n for d, n in enumerate(value.shape)]
+    full = lax.dynamic_update_slice_in_dim(
+        jnp.zeros(dims, value.dtype), value, here * step, axis=dim
+    )
+    going_up = going_down = value
+    for far in range(1, ways // 2 + 1):
+        going_up = lax.ppermute(going_up, axis, [(d, (d + 1) % ways) for d in range(ways)])
+        full = lax.dynamic_update_slice_in_dim(full, going_up, (here - far) % ways * step, axis=dim)
+        if 2 * far < ways:
+            going_down = lax.ppermute(going_down, axis, [(d, (d - 1) % ways) for d in range(ways)])
+            full = lax.dynamic_update_slice_in_dim(
+                full, going_down, (here + far) % ways * step, axis=dim
+            )
+    return full
 
 
 def prefix(shard, axis, combine, identity):
@@ -129,7 +147,7 @@
         )
     )
     carry = start_state
-    key_piece = lax.all_gather(k_soft, "seq", axis=0, tiled=True)
+    key_piece = collect(k_soft, "seq", 0)
     value_piece = lax.all_gather(v_soft, "seq", axis=0, tiled=True)
     piece_rows = key_piece.shape[0]
     blocks = piece_rows // half_rows

time: 393 us -> 381 us (0.969)
  waiting for transfers between devices: 150 us -> 58 us
  starting transfers between devices: 0.2 us -> 42.6 us
  local copies, waits for them, and re-layouts: 63.5 us -> 105 us
  blocking collectives: 43.7 us -> 38.6 us
    all_gather x1, waiting for transfers between devices: 58.2 us -> 0.02 us  [softmax_heads(): value_piece = lax.all_gather(v_soft, 'seq', axis=0, tiled=True)]
    all_gather x1 -> x0, waiting for transfers between devices: 43.7 us -> none  [softmax_heads(): key_piece = lax.all_gather(k_soft, 'seq', axis=0, tiled=True)]
    ppermute x0 -> x15, starting transfers between devices: none -> 42.5 us  [the longest x7 38.7 us: collect(): lax.ppermute(going_down, axis, [(d, (d - 1) % ways) for d in range(ways)])]
    squeeze x0 -> x32, local copies, waits for them, and re-layouts: none -> 27.6 us  [softmax_heads(): carry, _ = lax.scan(inner, carry, (key_blocks, value_blocks, firsts))]
    ppermute x0 -> x15, waiting for transfers between devices: none -> 22.5 us  [the longest x8 18.2 us: collect(): lax.ppermute(going_up, axis, [(d, (d + 1) % ways) for d in range(ways)])]
    dynamic_update_slice x0 -> x16, local copies, waits for them, and re-layouts: none -> 11 us  [the longest x8 5.51 us: collect(): lax.dynamic_update_slice_in_dim(full, going_up, (here - far) % ways * ste...]
    all_gather x1, waiting for transfers between devices: 8.65 us -> 0.01 us  [prefix(): lax.all_gather(part.astype(kind), axis)]
    unnamed x12 -> x19, local copies, waits for them, and re-layouts: 1.61 us -> 9.67 us
  transfers between devices with their start and end apart: 5 -> 19, of which waited for: 4 -> 11; matrix products, arithmetic and copies ran while one was open for 22% -> 34% of each run, Pallas kernels for 0% -> 0%
where the time goes in v1:
time: 381 us; the launch traced here: 375 us
  local copies, waits for them, and re-layouts  105 us (28%)
  loops' own time  88.5 us (23%)
  waiting for transfers between devices  58 us (15%)
  starting transfers between devices  42.6 us (11%)
  blocking collectives  38.6 us (10%)
  other arithmetic  16.8 us (4%)
  between operations  14.8 us (4%)
  matrix products  10.7 us (3%)
    another operation x1, loops' own time, softmax_heads(): carry, _ = lax.scan(inner, carry, (key_blocks, value_blocks, firsts))  85.2 us
    dynamic_slice x64, local copies, waits for them, and re-layouts, softmax_heads(): carry, _ = lax.scan(inner, carry, (key_blocks, value_blocks, firsts))  47.3 us
    ppermute x7, starting transfers between devices, collect(): lax.ppermute(going_down, axis, [(d, (d - 1) % ways) for d in range(ways)])  38.7 us
    unnamed x1, blocking collectives  38.6 us
    reduce_scatter x1, waiting for transfers between devices, local(): lax.psum_scatter(soft_term.astype(jnp.bfloat16).astype(jnp.float32).astyp...  35.3 us
    squeeze x32, local copies, waits for them, and re-layouts, softmax_heads(): carry, _ = lax.scan(inner, carry, (key_blocks, value_blocks, firsts))  27.6 us
    ppermute x8, waiting for transfers between devices, collect(): lax.ppermute(going_up, axis, [(d, (d + 1) % ways) for d in range(ways)])  18.2 us
    select_n x16, other arithmetic, turn(): return jax.tree.map(lambda a, b: jnp.where(reached, a, b), new, before)  14.9 us
  transfers between devices with their start and end apart: 19, of which 11 were waited for; matrix products, arithmetic and copies ran while one was open for 34% of the time, Pallas kernels for 0%

profile of v1, /device:TPU:0, one launch (start us, length us, event | category | flops | bytes accessed | tf_op | source)
XLA Modules:
  0.0 375.4 jit_solution(9353158057811611917)
XLA Ops:
  9.3 1.0 copy.96
  10.3 1.8 convolution_convert_fusion.2
  12.2 3.0 collective-permute-start
  15.2 4.1 %collective-permute-start.1 = (bf16[256,256]{1,0:T(8,128)(2,1)}, bf16[256,256]{1,0:T(8,128)(2,1)S(1)}, u32[]{:S(2)}, u32[]{:S(2)}) collective-permute-start(bf16[256,256]{1,0:T(8,128)(2,1)} %param.26), channel_id=1, source_target_pairs={{0,30},{2,0},{4,2},{6,4},{8,6},{10,8},{12,10},{14,12},{16,14},{18,... | collective-permute-start | bytes 393224 | tf_op jit(solution)/shard_map/ppermute | solution.py:22
  19.4 1.0 copy.65
  20.4 1.1 convolution_multiply_fusion.4
  21.6 1.6 broadcast_in_dim.66
  25.3 38.6 %all-reduce = bf16[32]{0:T(256)(128)(2,1)S(1)} all-reduce(bf16[32]{0:T(256)(128)(2,1)S(1)} %dynamic-update-slice), channel_id=2, replica_groups=mesh['seq'=16,'head'=2] {'seq'}, use_global_device_ids=true, to_apply=%add | all-reduce | flops 32 | bytes 128
  65.4 5.3 %collective-permute-start.3 = (bf16[256,256]{1,0:T(8,128)(2,1)S(1)}, bf16[256,256]{1,0:T(8,128)(2,1)S(1)}, u32[]{:S(2)}, u32[]{:S(2)}) collective-permute-start(bf16[256,256]{1,0:T(8,128)(2,1)S(1)} %collective-permute-done.1), channel_id=1, source_target_pairs={{0,30},{2,0},{4,2},{6,4},{8,6},{10,8},{12,10},{14,12},{16,14},{18,... | collective-permute-start | bytes 393224 | tf_op jit(solution)/shard_map/ppermute | solution.py:22
  71.4 1.9 collective-permute-done.2
  74.2 5.7 %collective-permute-start.5 = (bf16[256,256]{1,0:T(8,128)(2,1)S(1)}, bf16[256,256]{1,0:T(8,128)(2,1)S(1)}, u32[]{:S(2)}, u32[]{:S(2)}) collective-permute-start(bf16[256,256]{1,0:T(8,128)(2,1)S(1)} %collective-permute-done.3), channel_id=1, source_target_pairs={{0,30},{2,0},{4,2},{6,4},{8,6},{10,8},{12,10},{14,12},{16,14},{18,... | collective-permute-start | bytes 393224 | tf_op jit(solution)/shard_map/ppermute | solution.py:22
  80.6 2.9 collective-permute-done.4
  84.4 5.7 %collective-permute-start.7 = (bf16[256,256]{1,0:T(8,128)(2,1)S(1)}, bf16[256,256]{1,0:T(8,128)(2,1)S(1)}, u32[]{:S(2)}, u32[]{:S(2)}) collective-permute-start(bf16[256,256]{1,0:T(8,128)(2,1)S(1)} %collective-permute-done.5), channel_id=1, source_target_pairs={{0,30},{2,0},{4,2},{6,4},{8,6},{10,8},{12,10},{14,12},{16,14},{18,... | collective-permute-start | bytes 393224 | tf_op jit(solution)/shard_map/ppermute | solution.py:22
  90.8 3.3 collective-permute-done.6
  95.0 5.6 %collective-permute-start.9 = (bf16[256,256]{1,0:T(8,128)(2,1)S(1)}, bf16[256,256]{1,0:T(8,128)(2,1)S(1)}, u32[]{:S(2)}, u32[]{:S(2)}) collective-permute-start(bf16[256,256]{1,0:T(8,128)(2,1)S(1)} %collective-permute-done.7), channel_id=1, source_target_pairs={{0,30},{2,0},{4,2},{6,4},{8,6},{10,8},{12,10},{14,12},{16,14},{18,... | collective-permute-start | bytes 393224 | tf_op jit(solution)/shard_map/ppermute | solution.py:22
  101.4 1.5 collective-permute-done.8
  103.7 1.3 collective-permute-done.9
  105.1 6.2 %collective-permute-start.11 = (bf16[256,256]{1,0:T(8,128)(2,1)S(1)}, bf16[256,256]{1,0:T(8,128)(2,1)S(1)}, u32[]{:S(2)}, u32[]{:S(2)}) collective-permute-start(bf16[256,256]{1,0:T(8,128)(2,1)S(1)} %collective-permute-done.9), channel_id=1, source_target_pairs={{0,30},{2,0},{4,2},{6,4},{8,6},{10,8},{12,10},{14,12},{16,14},{18,... | collective-permute-start | bytes 393224 | tf_op jit(solution)/shard_map/ppermute | solution.py:22
  112.0 1.1 collective-permute-done.10
  114.3 6.2 %collective-permute-start.13 = (bf16[256,256]{1,0:T(8,128)(2,1)S(1)}, bf16[256,256]{1,0:T(8,128)(2,1)S(1)}, u32[]{:S(2)}, u32[]{:S(2)}) collective-permute-start(bf16[256,256]{1,0:T(8,128)(2,1)S(1)} %collective-permute-done.11), channel_id=1, source_target_pairs={{0,30},{2,0},{4,2},{6,4},{8,6},{10,8},{12,10},{14,12},{16,14},{18,... | collective-permute-start | bytes 393224 | tf_op jit(solution)/shard_map/ppermute | solution.py:22
  122.7 2.8 collective-permute-done.13
  126.3 6.9 %collective-permute-done.14 = bf16[256,256]{1,0:T(8,128)(2,1)S(1)} collective-permute-done((bf16[256,256]{1,0:T(8,128)(2,1)S(1)}, bf16[256,256]{1,0:T(8,128)(2,1)S(1)}, u32[]{:S(2)}, u32[]{:S(2)}) %collective-permute-start.14) | collective-permute-done | bytes 131104 | tf_op jit(solution)/shard_map/ppermute | solution.py:19
  134.0 3.4 copy.100
  137.4 4.3 %copy.82 = bf16[32,128,2,128]{3,1,2,0:T(8,128)(2,1)} copy(bf16[32,128,2,128]{1,0,3,2:T(8,128)(2,1)} %bitcast.140) | data formatting | bytes 4194304
  141.8 15.6 %while.39 = (s32[]{:T(128)}, f32[2,128,128]{2,1,0:T(8,128)S(1)}, s32[]{:T(128)}, bf16[16,2]{1,0:T(8,128)(2,1)S(1)}, bf16[16,2,128,128]{3,2,1,0:T(8,128)(2,1)}, /*index=5*/s32[]{:T(128)}, s32[]{:T(128)}) while((s32[]{:T(128)}, f32[2,128,128]{2,1,0:T(8,128)S(1)}, s32[]{:T(128)}, bf16[16,2]{1,0:T(8,128)(2,1)S(1)}, ...), condition=%wide.region_3.4_spmd.clone, body=%wide.region_2.3_spmd.clone.sunk | while | flops 163846 | bytes 327805 | solution.py:49
  141.8 1.0 fusion.77
  142.8 0.9 fusion.77
  143.8 0.9 fusion.77
  144.7 0.9 fusion.77
  145.7 0.9 fusion.77
  146.7 0.9 fusion.77
  147.6 0.9 fusion.77
  148.6 0.9 fusion.77
  149.6 0.9 fusion.77
  150.6 0.9 fusion.77
  151.5 0.9 fusion.77
  152.5 0.9 fusion.77
  153.5 0.9 fusion.77
  154.5 0.9 fusion.77
  155.4 0.9 fusion.77
  156.4 0.9 fusion.77
  158.2 2.1 convolution_convert_fusion.1
  160.4 4.1 %reshape.143 = bf16[32,128,2,128]{3,2,1,0:T(2,128)(2,1)} reshape(bf16[4096,256]{1,0:T(8,128)(2,1)} %all-gather.5.cloned.1.call-done) | data formatting | bytes 4194304 | tf_op jit(solution)/shard_map/reshape | solution.py:155
  164.5 165.0 %while.38 = (s32[]{:T(128)}, f32[2,128]{1,0:T(2,128)S(1)}, f32[2,128]{1,0:T(2,128)S(1)}, f32[128,2,128]{2,0,1:T(8,128)S(1)}, f32[2,128]{1,0:T(2,128)S(1)}, /*ind...) while((s32[]{:T(128)}, f32[2,128]{1,0:T(2,128)S(1)}, ...), condition=%wide.region_23.24_spmd.clone.clone, body=%wide.region_6.23_spmd.clone.clone.sunk | while | flops 34162200 | bytes 2179927 | solution.py:168
  167.7 0.9 constant_dynamic-slice_fusion.2
  179.5 0.9 constant_dynamic-slice_fusion.2
  329.8 3.7 convolution_convert_fusion
  333.5 35.3 %reduce-scatter.5.cloned.1.call-done = bf16[256,2048]{1,0:T(8,128)(2,1)} async-done(((bf16[256,4096]{1,0:T(8,128)(2,1)}), bf16[256,2048]{1,0:T(8,128)(2,1)}) %reduce-scatter.5.cloned.1.call-update) | async-done | bytes 1048592 | tf_op jit(solution)/shard_map/reduce_scatter | solution.py:191
  (386 shorter events, 100.1 us)
Async XLA Ops:
  7.2 151.0 %copy-start = (bf16[256,4096]{1,0:T(8,128)(2,1)S(1)}, bf16[256,4096]{1,0:T(8,128)(2,1)}, u32[]{:S(2)}) copy-start(bf16[256,4096]{1,0:T(8,128)(2,1)} %param.28) | copy-start | bytes 6291460
  7.2 134.6 %all-gather.7.cloned.1.call-start = ((), (), s32[]{:S(2)}) async-start(), calls=%async_computation.5 | async-start | bytes 1114112 | tf_op jit(solution)/shard_map/all_gather | solution.py:32
  12.2 148.2 %all-gather.5.cloned.1.call-start = ((), (), s32[]{:S(2)}) async-start(), calls=%async_computation.3 | async-start | bytes 2228224 | tf_op jit(solution)/shard_map/all_gather | solution.py:151
  12.2 51.8 %collective-permute-start = (bf16[256,256]{1,0:T(8,128)(2,1)}, bf16[256,256]{1,0:T(8,128)(2,1)S(1)}, u32[]{:S(2)}, u32[]{:S(2)}) collective-permute-start(bf16[256,256]{1,0:T(8,128)(2,1)} %param.26), channel_id=1, source_target_pairs={{0,2},{2,4},{4,6},{6,8},{8,10},{10,12},{12,14},{14,16},{16,18},{18... | collective-permute-start | bytes 393224 | tf_op jit(solution)/shard_map/ppermute | solution.py:19
  15.2 50.1 %collective-permute-start.1 = (bf16[256,256]{1,0:T(8,128)(2,1)}, bf16[256,256]{1,0:T(8,128)(2,1)S(1)}, u32[]{:S(2)}, u32[]{:S(2)}) collective-permute-start(bf16[256,256]{1,0:T(8,128)(2,1)} %param.26), channel_id=1, source_target_pairs={{0,30},{2,0},{4,2},{6,4},{8,6},{10,8},{12,10},{14,12},{16,14},{18,... | collective-permute-start | bytes 393224 | tf_op jit(solution)/shard_map/ppermute | solution.py:22
  19.3 4.5 %copy-start.2 = (bf16[256,256]{1,0:T(8,128)(2,1)S(1)}, bf16[256,256]{1,0:T(8,128)(2,1)}, u32[]{:S(2)}) copy-start(bf16[256,256]{1,0:T(8,128)(2,1)} %param.25) | copy-start | bytes 393220
  19.3 314.2 %reduce-scatter.3.cloned.1.call-start = ((), (), s32[]{:S(2)}) async-start(), calls=%async_computation.2 | async-start | bytes 3145728 | tf_op jit(solution)/shard_map/reduce_scatter | solution.py:185
  20.4 3.5 copy-start.4
  64.2 9.1 %collective-permute-start.2 = (bf16[256,256]{1,0:T(8,128)(2,1)S(1)}, bf16[256,256]{1,0:T(8,128)(2,1)S(1)}, u32[]{:S(2)}, u32[]{:S(2)}) collective-permute-start(bf16[256,256]{1,0:T(8,128)(2,1)S(1)} %collective-permute-done), channel_id=1, source_target_pairs={{0,2},{2,4},{4,6},{6,8},{8,10},{10,12},{12,14},{14,16},{16,18},{18... | collective-permute-start | bytes 393224 | tf_op jit(solution)/shard_map/ppermute | solution.py:19
  65.4 8.7 %collective-permute-start.3 = (bf16[256,256]{1,0:T(8,128)(2,1)S(1)}, bf16[256,256]{1,0:T(8,128)(2,1)S(1)}, u32[]{:S(2)}, u32[]{:S(2)}) collective-permute-start(bf16[256,256]{1,0:T(8,128)(2,1)S(1)} %collective-permute-done.1), channel_id=1, source_target_pairs={{0,30},{2,0},{4,2},{6,4},{8,6},{10,8},{12,10},{14,12},{16,14},{18,... | collective-permute-start | bytes 393224 | tf_op jit(solution)/shard_map/ppermute | solution.py:22
  73.4 10.1 %collective-permute-start.4 = (bf16[256,256]{1,0:T(8,128)(2,1)S(1)}, bf16[256,256]{1,0:T(8,128)(2,1)S(1)}, u32[]{:S(2)}, u32[]{:S(2)}) collective-permute-start(bf16[256,256]{1,0:T(8,128)(2,1)S(1)} %collective-permute-done.2), channel_id=1, source_target_pairs={{0,2},{2,4},{4,6},{6,8},{8,10},{10,12},{12,14},{14,16},{16,18},{18... | collective-permute-start | bytes 393224 | tf_op jit(solution)/shard_map/ppermute | solution.py:19
  74.2 10.1 %collective-permute-start.5 = (bf16[256,256]{1,0:T(8,128)(2,1)S(1)}, bf16[256,256]{1,0:T(8,128)(2,1)S(1)}, u32[]{:S(2)}, u32[]{:S(2)}) collective-permute-start(bf16[256,256]{1,0:T(8,128)(2,1)S(1)} %collective-permute-done.3), channel_id=1, source_target_pairs={{0,30},{2,0},{4,2},{6,4},{8,6},{10,8},{12,10},{14,12},{16,14},{18,... | collective-permute-start | bytes 393224 | tf_op jit(solution)/shard_map/ppermute | solution.py:22
  83.5 10.5 %collective-permute-start.6 = (bf16[256,256]{1,0:T(8,128)(2,1)S(1)}, bf16[256,256]{1,0:T(8,128)(2,1)S(1)}, u32[]{:S(2)}, u32[]{:S(2)}) collective-permute-start(bf16[256,256]{1,0:T(8,128)(2,1)S(1)} %collective-permute-done.4), channel_id=1, source_target_pairs={{0,2},{2,4},{4,6},{6,8},{8,10},{10,12},{12,14},{14,16},{16,18},{18... | collective-permute-start | bytes 393224 | tf_op jit(solution)/shard_map/ppermute | solution.py:19
  84.4 10.5 %collective-permute-start.7 = (bf16[256,256]{1,0:T(8,128)(2,1)S(1)}, bf16[256,256]{1,0:T(8,128)(2,1)S(1)}, u32[]{:S(2)}, u32[]{:S(2)}) collective-permute-start(bf16[256,256]{1,0:T(8,128)(2,1)S(1)} %collective-permute-done.5), channel_id=1, source_target_pairs={{0,30},{2,0},{4,2},{6,4},{8,6},{10,8},{12,10},{14,12},{16,14},{18,... | collective-permute-start | bytes 393224 | tf_op jit(solution)/shard_map/ppermute | solution.py:22
  94.1 8.7 %collective-permute-start.8 = (bf16[256,256]{1,0:T(8,128)(2,1)S(1)}, bf16[256,256]{1,0:T(8,128)(2,1)S(1)}, u32[]{:S(2)}, u32[]{:S(2)}) collective-permute-start(bf16[256,256]{1,0:T(8,128)(2,1)S(1)} %collective-permute-done.6), channel_id=1, source_target_pairs={{0,2},{2,4},{4,6},{6,8},{8,10},{10,12},{12,14},{14,16},{16,18},{18... | collective-permute-start | bytes 393224 | tf_op jit(solution)/shard_map/ppermute | solution.py:19
  95.0 10.0 %collective-permute-start.9 = (bf16[256,256]{1,0:T(8,128)(2,1)S(1)}, bf16[256,256]{1,0:T(8,128)(2,1)S(1)}, u32[]{:S(2)}, u32[]{:S(2)}) collective-permute-start(bf16[256,256]{1,0:T(8,128)(2,1)S(1)} %collective-permute-done.7), channel_id=1, source_target_pairs={{0,30},{2,0},{4,2},{6,4},{8,6},{10,8},{12,10},{14,12},{16,14},{18,... | collective-permute-start | bytes 393224 | tf_op jit(solution)/shard_map/ppermute | solution.py:22
  103.0 10.2 %collective-permute-start.10 = (bf16[256,256]{1,0:T(8,128)(2,1)S(1)}, bf16[256,256]{1,0:T(8,128)(2,1)S(1)}, u32[]{:S(2)}, u32[]{:S(2)}) collective-permute-start(bf16[256,256]{1,0:T(8,128)(2,1)S(1)} %collective-permute-done.8), channel_id=1, source_target_pairs={{0,2},{2,4},{4,6},{6,8},{8,10},{10,12},{12,14},{14,16},{16,18},{18... | collective-permute-start | bytes 393224 | tf_op jit(solution)/shard_map/ppermute | solution.py:19
  105.1 9.1 %collective-permute-start.11 = (bf16[256,256]{1,0:T(8,128)(2,1)S(1)}, bf16[256,256]{1,0:T(8,128)(2,1)S(1)}, u32[]{:S(2)}, u32[]{:S(2)}) collective-permute-start(bf16[256,256]{1,0:T(8,128)(2,1)S(1)} %collective-permute-done.9), channel_id=1, source_target_pairs={{0,30},{2,0},{4,2},{6,4},{8,6},{10,8},{12,10},{14,12},{16,14},{18,... | collective-permute-start | bytes 393224 | tf_op jit(solution)/shard_map/ppermute | solution.py:22
  113.2 8.6 %collective-permute-start.12 = (bf16[256,256]{1,0:T(8,128)(2,1)S(1)}, bf16[256,256]{1,0:T(8,128)(2,1)S(1)}, u32[]{:S(2)}, u32[]{:S(2)}) collective-permute-start(bf16[256,256]{1,0:T(8,128)(2,1)S(1)} %collective-permute-done.10), channel_id=1, source_target_pairs={{0,2},{2,4},{4,6},{6,8},{8,10},{10,12},{12,14},{14,16},{16,18},{18... | collective-permute-start | bytes 393224 | tf_op jit(solution)/shard_map/ppermute | solution.py:19
  114.3 11.1 %collective-permute-start.13 = (bf16[256,256]{1,0:T(8,128)(2,1)S(1)}, bf16[256,256]{1,0:T(8,128)(2,1)S(1)}, u32[]{:S(2)}, u32[]{:S(2)}) collective-permute-start(bf16[256,256]{1,0:T(8,128)(2,1)S(1)} %collective-permute-done.11), channel_id=1, source_target_pairs={{0,30},{2,0},{4,2},{6,4},{8,6},{10,8},{12,10},{14,12},{16,14},{18,... | collective-permute-start | bytes 393224 | tf_op jit(solution)/shard_map/ppermute | solution.py:22
  122.0 11.3 %collective-permute-start.14 = (bf16[256,256]{1,0:T(8,128)(2,1)S(1)}, bf16[256,256]{1,0:T(8,128)(2,1)S(1)}, u32[]{:S(2)}, u32[]{:S(2)}) collective-permute-start(bf16[256,256]{1,0:T(8,128)(2,1)S(1)} %collective-permute-done.12), channel_id=1, source_target_pairs={{0,2},{2,4},{4,6},{6,8},{8,10},{10,12},{12,14},{14,16},{16,18},{18... | collective-permute-start | bytes 393224 | tf_op jit(solution)/shard_map/ppermute | solution.py:19
  137.4 19.9 %copy-start.3 = (bf16[256,256]{1,0:T(8,128)(2,1)S(1)}, bf16[256,256]{1,0:T(8,128)(2,1)}, u32[]{:S(2)}) copy-start(bf16[256,256]{1,0:T(8,128)(2,1)} %param.21) | copy-start | bytes 393220
  141.8 15.9 %copy-start.1 = (bf16[256,256]{1,0:T(8,128)(2,1)S(1)}, bf16[256,256]{1,0:T(8,128)(2,1)}, u32[]{:S(2)}) copy-start(bf16[256,256]{1,0:T(8,128)(2,1)} %param.23) | copy-start | bytes 393220
  160.3 208.5 %reduce-scatter.5.cloned.1.call-start = ((), (), s32[]{:S(2)}) async-start(), calls=%async_computation.4 | async-start | bytes 3145728 | tf_op jit(solution)/shard_map/reduce_scatter | solution.py:191
Sparse Core Ops, SparseCore 0:
  12.3 60.2 all-gather.6
  75.3 63.9 all-gather.4
  160.4 5.4 reduce-scatter.2
  333.6 35.1 reduce-scatter.4
